TPU v7x, 32 devices: a whole 2x2x4 slice. The times are simulated.
32 devices in a mesh: src: 4 (over x, core), gx: 4 (over z), yz: 2 (over y).
Axes of the slice: x: 2, y: 2, z: 4, core: 2. Of those that a mesh axis runs over, the one named last changes fastest.
Arguments:
- warm_start: float32 [2, 16, 128, 32, 256], P(None, 'src', 'gx', 'yz'), may hold values from -1 to 1, as said below
- conductivity: float32 [128, 32, 256], P('gx', 'yz'), may hold values from 0.2 to 5
- currents: float32 [16], P('src'), may hold values from 4 to 16
- electrodes: int32 [16, 2], P('src'), may hold values from 0 to 1048575
- receivers: int32 [256], replicated, may hold values from 0 to 1048575
- weights: float32 [16, 256], P('src'), may hold values from -24 to 24
Outputs:
- solutions: float32 [2, 16, 128, 32, 256], P(None, 'src', 'gx', 'yz')
- gradient: float32 [128, 32, 256], P('gx', 'yz', 'src')
Inputs may be any that keep to these rules, and one draw needn't show every extreme that they name: `warm_start`: previous potentials, finite.
All inputs are finite; a program needn't handle non-finite values.
Results may differ from a plain program's by a relative error of at most 0.0003.
Values sent between devices are 32-bit elements; how exact they have to be, the bound alone decides.
A program may use at most 128 MiB of HBM per device.

v0:
```python
import functools
import jax
import jax.numpy as jnp
from jax import lax
from jax.experimental import pallas as pl
from jax.experimental.pallas import tpu as pltpu
from jax.sharding import PartitionSpec as P

MESH = pl.DeviceIdType.MESH
F32 = jnp.float32
COLS = 8
PAIRS = [(a, b) for a in range(COLS) for b in range(a, COLS)]


def matmul8(left, right):
    total = left[:, 0:1] * right[0:1, :]
    for k in range(1, COLS):
        total = total + left[:, k : k + 1] * right[k : k + 1, :]
    return total


def inverse8(matrix, row, lane):
    work = jnp.where(lane < COLS, matrix, jnp.where(lane - COLS == row, 1.0, 0.0))
    for k in range(COLS):
        scaled = work[k : k + 1, :] / work[k : k + 1, k : k + 1]
        work = jnp.where(row == k, scaled, work - work[:, k : k + 1] * scaled)
    return pltpu.roll(work, 128 - COLS, 1)


def kernel(
    sizes,
    warm, cond, currents, electrodes, receivers, weights,
    out_x, out_g,
    xv, pv, wv, yh, ysend, cv, ch, csend, cf, dv, iv, ybuf, onehot, table, gbuf, gp, grecv,
    load_sem, out_sem, send_sem, recv_sem, csend_sem, crecv_sem, gram_send, gram_recv, grad_send, grad_recv,
):
    nsrc, ngx, nyz, nx, ny, nz = sizes
    count = COLS // 2
    src, gx, yz = lax.axis_index("src"), lax.axis_index("gx"), lax.axis_index("yz")
    group = ngx * nyz
    me = gx * nyz + yz

    load_c = pltpu.make_async_copy(cond, cv.at[pl.ds(1, nx)], load_sem.at[0])
    load_x = pltpu.make_async_copy(warm, xv.at[:, pl.ds(1, nx)], load_sem.at[1])
    load_c.start()
    load_x.start()

    barrier = pltpu.get_barrier_semaphore()
    for o in range(1, group):
        to = lax.rem(me + o, group)
        pl.semaphore_signal(
            barrier, inc=1, device_id={"gx": to // nyz, "yz": lax.rem(to, nyz)}, device_id_type=MESH
        )
    for o in range(1, nsrc):
        pl.semaphore_signal(
            barrier, inc=1, device_id={"src": lax.rem(src + o, nsrc)}, device_id_type=MESH
        )

    edges = (gx > 0, gx < ngx - 1, yz > 0, yz < nyz - 1)
    fields = (xv, pv, wv)

    for side, plane in ((0, 0), (1, nx + 1)):
        @pl.when(jnp.logical_not(edges[side]))
        def _(plane=plane):
            cv[plane] = jnp.zeros((ny, nz), F32)
            for ref in fields:
                for c in range(COLS):
                    ref[c, plane] = jnp.zeros((ny, nz), F32)

    for side in (0, 1):
        @pl.when(jnp.logical_not(edges[2 + side]))
        def _(side=side):
            ch[side] = jnp.zeros((nx, nz), F32)
            for phase in range(3):
                for c in range(COLS):
                    yh[phase, side, c] = jnp.zeros((nx, nz), F32)

    def remote(source, target, send, recv, where):
        return pltpu.make_async_remote_copy(
            src_ref=source, dst_ref=target, send_sem=send, recv_sem=recv,
            device_id=where, device_id_type=MESH,
        )

    def x_copies(source, phase):
        def cut(plane):
            return source.at[plane] if phase == 3 else source.at[:, plane]
        if phase == 3:
            send, recv = csend_sem, crecv_sem
        else:
            send, recv = send_sem.at[phase], recv_sem.at[phase]
        return (
            (remote(cut(nx), cut(0), send.at[0], recv.at[0], {"gx": jnp.minimum(gx + 1, ngx - 1)}), edges[1], edges[0]),
            (remote(cut(1), cut(nx + 1), send.at[1], recv.at[1], {"gx": jnp.maximum(gx - 1, 0)}), edges[0], edges[1]),
        )

    def y_copies(phase):
        if phase == 3:
            send, recv, out, into = csend_sem, crecv_sem, csend, ch
        else:
            send, recv, out, into = send_sem.at[phase], recv_sem.at[phase], ysend.at[phase], yh.at[phase]
        return (
            (remote(out.at[1], into.at[0], send.at[2], recv.at[2], {"yz": jnp.minimum(yz + 1, nyz - 1)}), edges[3], edges[2]),
            (remote(out.at[0], into.at[1], send.at[3], recv.at[3], {"yz": jnp.maximum(yz - 1, 0)}), edges[2], edges[3]),
        )

    def start(copies):
        for copy, sends, _ in copies:
            pl.when(sends)(copy.start)

    def arrive(copies):
        for copy, _, receives in copies:
            pl.when(receives)(copy.wait_recv)

    def finish(copies):
        for copy, sends, _ in copies:
            pl.when(sends)(copy.wait_send)

    pl.semaphore_wait(barrier, group - 1 + nsrc - 1)

    load_c.wait()
    c_x = x_copies(cv, 3)
    start(c_x)
    for x in range(nx):
        csend[0, x : x + 1] = cv[x + 1, 0:1]
        csend[1, x : x + 1] = cv[x + 1, ny - 1 : ny]
    c_y = y_copies(3)
    start(c_y)

    load_x.wait()
    x_x = x_copies(xv, 0)

    @pl.loop(0, nx)
    def _(x):
        for c in range(COLS):
            ysend[0, 0, c, pl.ds(x, 1)] = xv[c, x + 1, 0:1]
            ysend[0, 1, c, pl.ds(x, 1)] = xv[c, x + 1, ny - 1 : ny]

    x_y = y_copies(0)
    start(x_y)
    start(x_x)

    row = lax.broadcasted_iota(jnp.int32, (ny, nz), 0)
    lane = lax.broadcasted_iota(jnp.int32, (ny, nz), 1)

    span = nyz * ny * nz
    place = receivers[...]
    where_x = place // span - gx * nx
    where_y = lax.rem(place, span) // nz - yz * ny
    inside = (where_x >= 0) & (where_x < nx) & (where_y >= 0) & (where_y < ny)
    line = jnp.where(inside, where_x * ny + where_y, -1)
    nrec = place.shape[1]
    spot = jnp.broadcast_to(lax.rem(place, nz), (nz, nrec))
    onehot[...] = jnp.where(
        lax.broadcasted_iota(jnp.int32, (nz, nrec), 0) == spot, 1.0, 0.0
    ).astype(jnp.bfloat16)
    step = 4
    rows = lax.broadcasted_iota(jnp.int32, (step * ny, nrec), 0)

    @pl.loop(0, nx // step)
    def _(i):
        match = rows + i * (step * ny) == line
        for s in range(count):
            value = weights[s : s + 1]
            total = None
            for part in range(3):
                piece = value.astype(jnp.bfloat16).astype(F32)
                value = value - piece
                term = lax.dot_general(
                    jnp.where(match, piece, 0.0).astype(jnp.bfloat16), onehot[...],
                    (((1,), (1,)), ((), ())), preferred_element_type=F32,
                )
                total = term if total is None else total + term
            for j in range(step):
                pv[count + s, i * step + j + 1] = total[j * ny : (j + 1) * ny]

    arrive(c_x)
    arrive(c_y)

    @pl.loop(0, nx)
    def _(x):
        mid = cv[x + 1]
        near = (
            cv[x + 2],
            cv[x],
            jnp.where(row == ny - 1, ch[1, pl.ds(x, 1)], pltpu.roll(mid, ny - 1, 0)),
            jnp.where(row == 0, ch[0, pl.ds(x, 1)], pltpu.roll(mid, 1, 0)),
            jnp.where(lane == nz - 1, 0.0, pltpu.roll(mid, nz - 1, 1)),
            jnp.where(lane == 0, 0.0, pltpu.roll(mid, 1, 1)),
        )
        faces = [0.5 * (mid + value) for value in near]
        diagonal = faces[0]
        for value in faces[1:]:
            diagonal = diagonal + value
        inverse = 1.0 / diagonal
        dv[x] = diagonal
        iv[x] = inverse
        faces[4] = jnp.where(lane == nz - 1, 0.0, faces[4])
        faces[5] = jnp.where(lane == 0, 0.0, faces[5])
        for j in range(6):
            cf[j, x] = faces[j] * inverse

    def around(phase, c, x):
        ref = fields[phase]
        field = ref[c, x + 1]
        above = jnp.where(row == ny - 1, yh[phase, 1, c, pl.ds(x, 1)], pltpu.roll(field, ny - 1, 0))
        below = jnp.where(row == 0, yh[phase, 0, c, pl.ds(x, 1)], pltpu.roll(field, 1, 0))
        total = cf[0, x] * ref[c, x + 2] + cf[1, x] * ref[c, x]
        total = total + cf[2, x] * above
        total = total + cf[3, x] * below
        total = total + cf[4, x] * pltpu.roll(field, nz - 1, 1)
        total = total + cf[5, x] * pltpu.roll(field, 1, 1)
        return field, total

    arrive(x_x)
    arrive(x_y)

    @pl.loop(0, nx)
    def _(x):
        cell = row * nz + lane + ((gx * nx + x) * span + yz * (ny * nz))
        inverse = iv[x]
        for c in range(COLS):
            field, total = around(0, c, x)
            if c < count:
                amount = currents[c]
                source = jnp.where(cell == electrodes[c, 0], amount, 0.0) - jnp.where(
                    cell == electrodes[c, 1], amount, 0.0
                )
            else:
                source = pv[c, x + 1]
            value = source * inverse - field + total
            pv[c, x + 1] = value
            ysend[1, 0, c, pl.ds(x, 1)] = value[0:1]
            ysend[1, 1, c, pl.ds(x, 1)] = value[ny - 1 : ny]

    p_x, p_y = x_copies(pv, 1), y_copies(1)
    start(p_y)
    start(p_x)

    def products(acc, x, left, right):
        acc = list(acc)
        for yb in range(ny // 8):
            for zb in range(nz // 128):
                cut = (slice(yb * 8, yb * 8 + 8), slice(zb * 128, zb * 128 + 128))
                scale = dv[(x,) + cut]
                lefts = [left[(a, x + 1) + cut] * scale for a in range(COLS)]
                if right is ybuf:
                    rights = [right[(b,) + cut] for b in range(COLS)]
                else:
                    rights = [right[(b, x + 1) + cut] for b in range(COLS)]
                for i, (a, b) in enumerate(PAIRS):
                    acc[i] = acc[i] + lefts[a] * rights[b]
        return tuple(acc)

    zeros = tuple(jnp.zeros((8, 128), F32) for _ in PAIRS)
    row8 = lax.broadcasted_iota(jnp.int32, (8, 128), 0)
    lane8 = lax.broadcasted_iota(jnp.int32, (8, 128), 1)

    def collect(acc):
        sums = {}
        for (a, b), value in zip(PAIRS, acc):
            sums[a, b] = sums[b, a] = jnp.sum(value, axis=0, keepdims=True)
        matrix = jnp.zeros((8, 128), F32)
        for a in range(COLS):
            block = jnp.zeros((8, 128), F32)
            for b in range(COLS):
                block = jnp.where(row8 == b, sums[a, b], block)
            matrix = jnp.where(lane8 == a, jnp.sum(block, axis=1, keepdims=True), matrix)
        return matrix

    def gram(left, right):
        return collect(lax.fori_loop(0, nx, lambda x, acc: products(acc, x, left, right), zeros))

    mine = gram(pv, pv)

    arrive(p_x)
    arrive(p_y)

    @pl.loop(0, nx)
    def _(x):
        for c in range(COLS):
            field, total = around(1, c, x)
            value = field - total
            wv[c, x + 1] = value
            ysend[2, 0, c, pl.ds(x, 1)] = value[0:1]
            ysend[2, 1, c, pl.ds(x, 1)] = value[ny - 1 : ny]

    w_x, w_y = x_copies(wv, 2), y_copies(2)
    start(w_y)
    start(w_x)

    mine = mine + pltpu.roll(gram(pv, wv), 8, 1)
    mine = mine + pltpu.roll(gram(wv, wv), 16, 1)

    arrive(w_x)
    arrive(w_y)

    def last(x, acc):
        for c in range(COLS):
            field, total = around(2, c, x)
            ybuf[c] = field - total
        return products(acc, x, wv, ybuf)

    mine = mine + pltpu.roll(collect(lax.fori_loop(0, nx, last, zeros)), 24, 1)

    gbuf[me] = mine
    sums = []
    for o in range(1, group):
        to = lax.rem(me + o, group)
        copy = remote(
            gbuf.at[me], gbuf.at[me], gram_send.at[o - 1], gram_recv.at[o - 1],
            {"gx": to // nyz, "yz": lax.rem(to, nyz)},
        )
        copy.start()
        sums.append(copy)
    for copy in sums:
        copy.wait_recv()
    total = gbuf[0]
    for o in range(1, group):
        total = total + gbuf[o]

    first = total
    curve = pltpu.roll(total, 120, 1)
    second = pltpu.roll(total, 112, 1)
    third = pltpu.roll(total, 104, 1)
    unit = jnp.where(row8 == lane8, 1.0, 0.0)
    curve_inv = inverse8(curve, row8, lane8)
    first_inv = inverse8(first, row8, lane8)
    alpha = matmul8(curve_inv, first)
    alpha_t = matmul8(first, curve_inv)
    second_alpha = matmul8(second, alpha)
    fresh = first - matmul8(curve, alpha) - matmul8(alpha_t, curve) + matmul8(alpha_t, second_alpha)
    mixed = unit + matmul8(first_inv, fresh)
    mixed_t = unit + matmul8(fresh, first_inv)
    upper = matmul8(curve, mixed) - second_alpha
    lower = matmul8(second, mixed) - matmul8(third, alpha)
    curve_next = matmul8(mixed_t, upper) - matmul8(alpha_t, lower)
    alpha_next = matmul8(inverse8(curve_next, row8, lane8), fresh)
    coef_p = alpha + matmul8(mixed, alpha_next)
    coef_w = -matmul8(alpha, alpha_next)
    for a in range(COLS):
        for b in range(COLS):
            table[a * COLS + b] = jnp.broadcast_to(coef_p[a : a + 1, b : b + 1], (8, 128))
            table[(COLS + a) * COLS + b] = jnp.broadcast_to(coef_w[a : a + 1, b : b + 1], (8, 128))

    def combine(xref, pref, wref, index, cuts):
        starts = [[ref[(a,) + index + cut] for a in range(COLS) for cut in cuts] for ref in (pref, wref)]
        n = len(cuts)
        for b in range(COLS):
            acc = [xref[(b,) + index + cut] for cut in cuts]
            for part in range(2):
                for a in range(COLS):
                    factor = table[(part * COLS + a) * COLS + b]
                    acc = [acc[j] + starts[part][a * n + j] * factor for j in range(n)]
            for j, cut in enumerate(cuts):
                xref[(b,) + index + cut] = acc[j]

    finish(x_x)
    lanes = [slice(zb * 128, zb * 128 + 128) for zb in range(nz // 128)]

    @pl.loop(0, nx + 2)
    def _(x):
        for yb in range(ny // 8):
            combine(xv, pv, wv, (x,), [(slice(yb * 8, yb * 8 + 8), cut) for cut in lanes])

    for side in (0, 1):
        @pl.when(edges[2 + side])
        def _(side=side):
            @pl.loop(0, nx // 8)
            def _(i):
                combine(
                    yh.at[0, side], yh.at[1, side], yh.at[2, side], (),
                    [(pl.ds(pl.multiple_of(i * 8, 8), 8), cut) for cut in lanes],
                )

    store_x = pltpu.make_async_copy(xv.at[:, pl.ds(1, nx)], out_x, out_sem)

    store_x.start()

    half = lane8 < 64
    chunks = 2
    length = nx // chunks
    sent = []

    def face(x):
        total = None
        for s in range(count):
            term = (xv[s, x] - xv[s, x + 1]) * (xv[count + s, x] - xv[count + s, x + 1])
            total = term if total is None else total + term
        return total

    def planes(x, before):
        after = face(x + 1)
        fy = fz = edge_y = edge_z = None
        for s in range(count):
            u, w = xv[s, x + 1], xv[count + s, x + 1]
            uy = u - jnp.where(row == ny - 1, yh[0, 1, s, pl.ds(x, 1)], pltpu.roll(u, ny - 1, 0))
            wy = w - jnp.where(row == ny - 1, yh[0, 1, count + s, pl.ds(x, 1)], pltpu.roll(w, ny - 1, 0))
            uz = u - jnp.where(lane == nz - 1, 0.0, pltpu.roll(u, nz - 1, 1))
            wz = w - jnp.where(lane == nz - 1, 0.0, pltpu.roll(w, nz - 1, 1))
            low = (u[0:1] - yh[0, 0, s, pl.ds(x, 1)]) * (w[0:1] - yh[0, 0, count + s, pl.ds(x, 1)])
            terms = (uy * wy, uz * wz, low, u * w)
            if fy is None:
                fy, fz, edge_y, edge_z = terms
            else:
                fy, fz, edge_y, edge_z = (p + q for p, q in zip((fy, fz, edge_y, edge_z), terms))
        total = before + after
        total = total + fy + jnp.where(row == 0, edge_y, pltpu.roll(fy, 1, 0))
        total = total + fz + jnp.where(lane == 0, edge_z, pltpu.roll(fz, 1, 1))
        total = -0.5 * total
        for t in range(nz // 128):
            top, low = total[0:8, lanes[t]], total[8:16, lanes[t]]
            gp[2 * t, x] = jnp.where(half, top, pltpu.roll(low, 64, 1))
            gp[2 * t + 1, x] = jnp.where(half, pltpu.roll(top, 64, 1), low)
        return after

    before = face(0)
    for k in range(chunks):
        before = lax.fori_loop(k * length, (k + 1) * length, planes, before)
        for o in range(1, nsrc):
            to = lax.rem(src + o, nsrc)
            part = pl.ds(k * length, length)
            copy = remote(
                gp.at[to, part], grecv.at[o - 1, part],
                grad_send.at[k, o - 1], grad_recv.at[k, o - 1], {"src": to},
            )
            copy.start()
            sent.append(copy)

    for k in range(chunks):
        for o in range(1, nsrc):
            sent[k * (nsrc - 1) + o - 1].wait_recv()

        @pl.loop(k * length, (k + 1) * length)
        def _(x):
            total = gp[src, x]
            for o in range(nsrc - 1):
                total = total + grecv[o, x]
            out_g[x, 0:8] = total[:, 0:64]
            out_g[x, 8:16] = pltpu.roll(total, 64, 1)[:, 0:64]

    for copies in (c_x, c_y, x_y, p_x, p_y, w_x, w_y):
        finish(copies)
    for copy in sums + sent:
        copy.wait_send()
    store_x.wait()


def on_device(sizes, warm_start, conductivity, currents, electrodes, receivers, weights):
    nsrc, ngx, nyz, nx, ny, nz = sizes
    group = ngx * nyz
    nrec = receivers.shape[0]
    dma = pltpu.SemaphoreType.DMA
    vmem = pl.BlockSpec(memory_space=pltpu.VMEM)
    smem = pl.BlockSpec(memory_space=pltpu.SMEM)
    hbm = pl.BlockSpec(memory_space=pl.ANY)
    block = pltpu.VMEM((COLS, nx + 2, ny, nz), F32)
    cells = COLS * nx * ny * nz
    solutions, gradient = pl.pallas_call(
        functools.partial(kernel, sizes),
        out_shape=(
            jax.ShapeDtypeStruct((COLS, nx, ny, nz), F32),
            jax.ShapeDtypeStruct((nx, ny, nz // nsrc), F32),
        ),
        in_specs=[hbm, hbm, smem, smem, vmem, vmem],
        out_specs=(hbm, vmem),
        scratch_shapes=[
            block, block, block,
            pltpu.VMEM((3, 2, COLS, nx, nz), F32),
            pltpu.VMEM((3, 2, COLS, nx, nz), F32),
            pltpu.VMEM((nx + 2, ny, nz), F32),
            pltpu.VMEM((2, nx, nz), F32),
            pltpu.VMEM((2, nx, nz), F32),
            pltpu.VMEM((6, nx, ny, nz), F32),
            pltpu.VMEM((nx, ny, nz), F32),
            pltpu.VMEM((nx, ny, nz), F32),
            pltpu.VMEM((COLS, ny, nz), F32),
            pltpu.VMEM((nz, nrec), jnp.bfloat16),
            pltpu.VMEM((2 * COLS * COLS, 8, 128), F32),
            pltpu.VMEM((group, 8, 128), F32),
            pltpu.VMEM((nsrc, nx, 8, 128), F32),
            pltpu.VMEM((nsrc - 1, nx, 8, 128), F32),
            dma((2,)), dma,
            dma((3, 4)), dma((3, 4)),
            dma((4,)), dma((4,)),
            dma((group - 1,)), dma((group - 1,)),
            dma((2, nsrc - 1)), dma((2, nsrc - 1)),
        ],
        compiler_params=pltpu.CompilerParams(
            collective_id=0, has_side_effects=True, vmem_limit_bytes=48 * 1024 * 1024
        ),
        cost_estimate=pl.CostEstimate(flops=300 * cells, bytes_accessed=8 * cells, transcendentals=0),
    )(
        warm_start.reshape((COLS, nx, ny, nz)), conductivity, currents, electrodes,
        receivers.reshape(1, nrec), weights,
    )
    return solutions.reshape(warm_start.shape), gradient


def solution(mesh):
    nsrc, ngx, nyz = (mesh.shape[name] for name in ("src", "gx", "yz"))

    def run(warm_start, conductivity, *rest):
        gx, gy, gz = conductivity.shape
        sizes = (nsrc, ngx, nyz, gx // ngx, gy // nyz, gz)
        return jax.shard_map(
            functools.partial(on_device, sizes),
            mesh=mesh,
            in_specs=(
                P(None, "src", "gx", "yz", None),
                P("gx", "yz", None),
                P("src"),
                P("src", None),
                P(),
                P("src", None),
            ),
            out_specs=(P(None, "src", "gx", "yz", None), P("gx", "yz", "src")),
            check_vma=False,
        )(warm_start, conductivity, *rest)

    return run
```

profile of v0, /device:TPU:0, one launch (start us, length us, event | category | flops | bytes accessed | tf_op | source)
XLA Modules:
  0.0 76.7 jit_solution(2297855303695997095)
XLA Ops:
  0.6 0.8 copy.8.electrodes
  1.4 0.0 copy-start
  1.4 1.0 %copy-done = f32[32,16,256]{2,1,0:T(8,128)S(1)} copy-done((f32[32,16,256]{2,1,0:T(8,128)S(1)}, f32[32,16,256]{2,1,0:T(8,128)}, u32[]{:S(2)}) %copy-start) | copy-done | bytes 524312
  2.4 0.0 copy-start.1
  2.4 0.7 copy-done.1
  3.1 0.0 copy-start.2
  3.1 0.7 copy-done.2
  3.8 0.0 copy-start.3
  3.8 0.7 copy-done.3
  4.5 69.5 %shard_map.77 = (f32[8,32,16,256]{3,2,1,0:T(8,128)S(1)}, f32[32,16,64]{2,1,0:T(8,128)S(1)}) custom-call(f32[8,32,16,256]{3,2,1,0:T(8,128)} %bitcast.5, f32[32,16,256]{2,1,0:T(8,128)S(1)} %copy-done, f32[4]{0:T(128)S(1)} %copy-done.3, s32[4,2]{1,0:T(4,128)S(1)} %copy.8.electrodes, s32[1,256]{1,0:T(1,128)S(1)} %bitcast.4, f32[4,256]{1,0:T(4,128)S(1)} %copy-done.1), custom_call_target="tpu_custom_call" | custom-call | flops 314572800 | bytes 8388608 | tf_op jit(solution)/shard_map/pallas_call | solution.py:458
  74.0 2.0 %copy.11 = f32[2,4,32,16,256]{4,3,2,1,0:T(8,128)} copy(f32[2,4,32,16,256]{4,3,2,1,0:T(8,128)S(1)} %bitcast.3) | data formatting | bytes 8388608
  76.0 0.7 copy.12
Async XLA Ops:
  1.4 1.0 %copy-start = (f32[32,16,256]{2,1,0:T(8,128)S(1)}, f32[32,16,256]{2,1,0:T(8,128)}, u32[]{:S(2)}) copy-start(f32[32,16,256]{2,1,0:T(8,128)} %cond.1) | copy-start | bytes 1572868
  2.4 0.7 copy-start.1
  3.1 0.7 copy-start.2
  3.8 0.7 copy-start.3
where the time goes:
time: 77 us; the launch traced here: 76.7 us
  Pallas kernels  69.5 us (90%)
  local copies, waits for them, and re-layouts  6.54 us (8%)
    pallas_call x1, Pallas kernels, on_device(): pl.pallas_call(functools.partial(kernel, sizes), out_shape=(jax.ShapeDtyp...  69.5 us
    unnamed x11, local copies, waits for them, and re-layouts  6.54 us

commit v1 on v0

--- a/solution.py
+++ b/solution.py
@@ -29,10 +29,11 @@
 
 def kernel(
     sizes,
-    warm, cond, currents, electrodes, receivers, weights,
+    warm, cond, currents_in, electrodes_in, receivers_in, weights_in,
     out_x, out_g,
+    currents, electrodes, receivers, weights,
     xv, pv, wv, yh, ysend, cv, ch, csend, cf, dv, iv, ybuf, onehot, table, gbuf, gp, grecv,
-    load_sem, out_sem, send_sem, recv_sem, csend_sem, crecv_sem, gram_send, gram_recv, grad_send, grad_recv,
+    load_sem, out_sem, send_sem, recv_sem, ysend_sem, yrecv_sem, csend_sem, crecv_sem, gram_send, gram_recv, grad_send, grad_recv,
 ):
     nsrc, ngx, nyz, nx, ny, nz = sizes
     count = COLS // 2
@@ -42,7 +43,15 @@
 
     load_c = pltpu.make_async_copy(cond, cv.at[pl.ds(1, nx)], load_sem.at[0])
     load_x = pltpu.make_async_copy(warm, xv.at[:, pl.ds(1, nx)], load_sem.at[1])
+    small = [
+        pltpu.make_async_copy(source, target, load_sem.at[2 + i])
+        for i, (source, target) in enumerate((
+            (currents_in, currents), (electrodes_in, electrodes), (receivers_in, receivers), (weights_in, weights),
+        ))
+    ]
     load_c.start()
+    for copy in small:
+        copy.start()
     load_x.start()
 
     barrier = pltpu.get_barrier_semaphore()
@@ -58,6 +67,8 @@
 
     edges = (gx > 0, gx < ngx - 1, yz > 0, yz < nyz - 1)
     fields = (xv, pv, wv)
+    parts = 4
+    width = nx // parts
 
     for side, plane in ((0, 0), (1, nx + 1)):
         @pl.when(jnp.logical_not(edges[side]))
@@ -84,24 +95,64 @@
     def x_copies(source, phase):
         def cut(plane):
             return source.at[plane] if phase == 3 else source.at[:, plane]
+
+        def mine(plane):
+            return warm.at[:, plane - 1] if phase == 0 else cut(plane)
         if phase == 3:
             send, recv = csend_sem, crecv_sem
         else:
             send, recv = send_sem.at[phase], recv_sem.at[phase]
         return (
-            (remote(cut(nx), cut(0), send.at[0], recv.at[0], {"gx": jnp.minimum(gx + 1, ngx - 1)}), edges[1], edges[0]),
-            (remote(cut(1), cut(nx + 1), send.at[1], recv.at[1], {"gx": jnp.maximum(gx - 1, 0)}), edges[0], edges[1]),
-        )
-
-    def y_copies(phase):
-        if phase == 3:
-            send, recv, out, into = csend_sem, crecv_sem, csend, ch
-        else:
-            send, recv, out, into = send_sem.at[phase], recv_sem.at[phase], ysend.at[phase], yh.at[phase]
+            (remote(mine(nx), cut(0), send.at[0], recv.at[0], {"gx": jnp.minimum(gx + 1, ngx - 1)}), edges[1], edges[0]),
+            (remote(mine(1), cut(nx + 1), send.at[1], recv.at[1], {"gx": jnp.maximum(gx - 1, 0)}), edges[0], edges[1]),
+        )
+
+    after_y, before_y = {"yz": jnp.minimum(yz + 1, nyz - 1)}, {"yz": jnp.maximum(yz - 1, 0)}
+
+    def c_copies():
         return (
-            (remote(out.at[1], into.at[0], send.at[2], recv.at[2], {"yz": jnp.minimum(yz + 1, nyz - 1)}), edges[3], edges[2]),
-            (remote(out.at[0], into.at[1], send.at[3], recv.at[3], {"yz": jnp.maximum(yz - 1, 0)}), edges[2], edges[3]),
-        )
+            (remote(csend.at[1], ch.at[0], csend_sem.at[2], crecv_sem.at[2], after_y), edges[3], edges[2]),
+            (remote(csend.at[0], ch.at[1], csend_sem.at[3], crecv_sem.at[3], before_y), edges[2], edges[3]),
+        )
+
+    def y_copies(phase, q):
+        part = pl.ds(pl.multiple_of(q * width, 8), width)
+        out, into = ysend.at[phase], yh.at[phase]
+        send, recv = ysend_sem.at[phase, q], yrecv_sem.at[phase, q]
+        return (
+            (remote(out.at[1, :, part], into.at[0, :, part], send.at[0], recv.at[0], after_y), edges[3], edges[2]),
+            (remote(out.at[0, :, part], into.at[1, :, part], send.at[1], recv.at[1], before_y), edges[2], edges[3]),
+        )
+
+    def sweep(phase, plane, carry):
+        def part(k, carry):
+            q = lax.rem(parts - k, parts)
+            arrive(y_copies(phase, q))
+            source = fields[phase]
+
+            @pl.when(k == 0)
+            def _():
+                arrive(x_copies(source, phase)[:1])
+
+            @pl.when(k == 1)
+            def _():
+                arrive(x_copies(source, phase)[1:])
+
+            carry = lax.fori_loop(0, width, lambda i, c: plane(q * width + i, c), carry)
+            if phase < 2:
+                start(y_copies(phase + 1, q))
+                target = fields[phase + 1]
+
+                @pl.when(k == 0)
+                def _():
+                    start(x_copies(target, phase + 1)[1:])
+
+                @pl.when(k == 1)
+                def _():
+                    start(x_copies(target, phase + 1)[:1])
+            return carry
+
+        return lax.fori_loop(0, parts, part, carry)
 
     def start(copies):
         for copy, sends, _ in copies:
@@ -117,17 +168,18 @@
 
     pl.semaphore_wait(barrier, group - 1 + nsrc - 1)
 
+    x_x = x_copies(xv, 0)
+    start(x_x)
     load_c.wait()
     c_x = x_copies(cv, 3)
     start(c_x)
     for x in range(nx):
         csend[0, x : x + 1] = cv[x + 1, 0:1]
         csend[1, x : x + 1] = cv[x + 1, ny - 1 : ny]
-    c_y = y_copies(3)
+    c_y = c_copies()
     start(c_y)
 
     load_x.wait()
-    x_x = x_copies(xv, 0)
 
     @pl.loop(0, nx)
     def _(x):
@@ -135,9 +187,10 @@
             ysend[0, 0, c, pl.ds(x, 1)] = xv[c, x + 1, 0:1]
             ysend[0, 1, c, pl.ds(x, 1)] = xv[c, x + 1, ny - 1 : ny]
 
-    x_y = y_copies(0)
-    start(x_y)
-    start(x_x)
+    for q in (0, 3, 2, 1):
+        start(y_copies(0, q))
+    for copy in small:
+        copy.wait()
 
     row = lax.broadcasted_iota(jnp.int32, (ny, nz), 0)
     lane = lax.broadcasted_iota(jnp.int32, (ny, nz), 1)
@@ -159,19 +212,20 @@
     @pl.loop(0, nx // step)
     def _(i):
         match = rows + i * (step * ny) == line
+        values = [weights[s : s + 1] for s in range(count)]
+        total = None
+        for part in range(2):
+            pieces = [value.astype(jnp.bfloat16).astype(F32) for value in values]
+            values = [value - piece for value, piece in zip(values, pieces)]
+            term = lax.dot_general(
+                jnp.concatenate([jnp.where(match, piece, 0.0).astype(jnp.bfloat16) for piece in pieces], axis=0),
+                onehot[...], (((1,), (1,)), ((), ())), preferred_element_type=F32,
+            )
+            total = term if total is None else total + term
         for s in range(count):
-            value = weights[s : s + 1]
-            total = None
-            for part in range(3):
-                piece = value.astype(jnp.bfloat16).astype(F32)
-                value = value - piece
-                term = lax.dot_general(
-                    jnp.where(match, piece, 0.0).astype(jnp.bfloat16), onehot[...],
-                    (((1,), (1,)), ((), ())), preferred_element_type=F32,
-                )
-                total = term if total is None else total + term
             for j in range(step):
-                pv[count + s, i * step + j + 1] = total[j * ny : (j + 1) * ny]
+                first = (s * step + j) * ny
+                pv[count + s, i * step + j + 1] = total[first : first + ny]
 
     arrive(c_x)
     arrive(c_y)
@@ -211,19 +265,15 @@
         total = total + cf[5, x] * pltpu.roll(field, 1, 1)
         return field, total
 
-    arrive(x_x)
-    arrive(x_y)
-
-    @pl.loop(0, nx)
-    def _(x):
+    def plane_p(x, carry):
         cell = row * nz + lane + ((gx * nx + x) * span + yz * (ny * nz))
         inverse = iv[x]
         for c in range(COLS):
             field, total = around(0, c, x)
             if c < count:
                 amount = currents[c]
-                source = jnp.where(cell == electrodes[c, 0], amount, 0.0) - jnp.where(
-                    cell == electrodes[c, 1], amount, 0.0
+                source = jnp.where(cell == electrodes[0, c], amount, 0.0) - jnp.where(
+                    cell == electrodes[1, c], amount, 0.0
                 )
             else:
                 source = pv[c, x + 1]
@@ -232,9 +282,9 @@
             ysend[1, 0, c, pl.ds(x, 1)] = value[0:1]
             ysend[1, 1, c, pl.ds(x, 1)] = value[ny - 1 : ny]
 
-    p_x, p_y = x_copies(pv, 1), y_copies(1)
-    start(p_y)
-    start(p_x)
+        return carry
+
+    sweep(0, plane_p, 0)
 
     def products(acc, x, left, right):
         acc = list(acc)
@@ -272,11 +322,7 @@
 
     mine = gram(pv, pv)
 
-    arrive(p_x)
-    arrive(p_y)
-
-    @pl.loop(0, nx)
-    def _(x):
+    def plane_w(x, carry):
         for c in range(COLS):
             field, total = around(1, c, x)
             value = field - total
@@ -284,15 +330,12 @@
             ysend[2, 0, c, pl.ds(x, 1)] = value[0:1]
             ysend[2, 1, c, pl.ds(x, 1)] = value[ny - 1 : ny]
 
-    w_x, w_y = x_copies(wv, 2), y_copies(2)
-    start(w_y)
-    start(w_x)
+        return carry
+
+    sweep(1, plane_w, 0)
 
     mine = mine + pltpu.roll(gram(pv, wv), 8, 1)
     mine = mine + pltpu.roll(gram(wv, wv), 16, 1)
-
-    arrive(w_x)
-    arrive(w_y)
 
     def last(x, acc):
         for c in range(COLS):
@@ -300,7 +343,7 @@
             ybuf[c] = field - total
         return products(acc, x, wv, ybuf)
 
-    mine = mine + pltpu.roll(collect(lax.fori_loop(0, nx, last, zeros)), 24, 1)
+    mine = mine + pltpu.roll(collect(sweep(2, last, zeros)), 24, 1)
 
     gbuf[me] = mine
     sums = []
@@ -377,9 +420,8 @@
     store_x.start()
 
     half = lane8 < 64
-    chunks = 2
+    chunks = 8
     length = nx // chunks
-    sent = []
 
     def face(x):
         total = None
@@ -413,34 +455,46 @@
             gp[2 * t + 1, x] = jnp.where(half, pltpu.roll(top, 64, 1), low)
         return after
 
-    before = face(0)
-    for k in range(chunks):
-        before = lax.fori_loop(k * length, (k + 1) * length, planes, before)
+    def grad_copies(k):
+        part = pl.ds(k * length, length)
         for o in range(1, nsrc):
             to = lax.rem(src + o, nsrc)
-            part = pl.ds(k * length, length)
-            copy = remote(
+            yield remote(
                 gp.at[to, part], grecv.at[o - 1, part],
                 grad_send.at[k, o - 1], grad_recv.at[k, o - 1], {"src": to},
             )
+
+    def send_chunk(k, before):
+        before = lax.fori_loop(k * length, (k + 1) * length, planes, before)
+        for copy in grad_copies(k):
             copy.start()
-            sent.append(copy)
-
-    for k in range(chunks):
-        for o in range(1, nsrc):
-            sent[k * (nsrc - 1) + o - 1].wait_recv()
-
-        @pl.loop(k * length, (k + 1) * length)
-        def _(x):
+        return before
+
+    lax.fori_loop(0, chunks, send_chunk, face(0))
+
+    @pl.loop(0, chunks)
+    def _(k):
+        for copy in grad_copies(k):
+            copy.wait_recv()
+        for i in range(length):
+            x = k * length + i
             total = gp[src, x]
             for o in range(nsrc - 1):
                 total = total + grecv[o, x]
             out_g[x, 0:8] = total[:, 0:64]
             out_g[x, 8:16] = pltpu.roll(total, 64, 1)[:, 0:64]
 
-    for copies in (c_x, c_y, x_y, p_x, p_y, w_x, w_y):
+    @pl.loop(0, chunks)
+    def _(k):
+        for copy in grad_copies(k):
+            copy.wait_send()
+
+    for copies in (c_x, c_y, x_copies(pv, 1), x_copies(wv, 2)):
         finish(copies)
-    for copy in sums + sent:
+    for phase in range(3):
+        for q in range(parts):
+            finish(y_copies(phase, q))
+    for copy in sums:
         copy.wait_send()
     store_x.wait()
 
@@ -449,10 +503,10 @@
     nsrc, ngx, nyz, nx, ny, nz = sizes
     group = ngx * nyz
     nrec = receivers.shape[0]
+    count = weights.shape[0]
     dma = pltpu.SemaphoreType.DMA
     vmem = pl.BlockSpec(memory_space=pltpu.VMEM)
-    smem = pl.BlockSpec(memory_space=pltpu.SMEM)
-    hbm = pl.BlockSpec(memory_space=pl.ANY)
+    hbm = pl.BlockSpec(memory_space=pltpu.HBM)
     block = pltpu.VMEM((COLS, nx + 2, ny, nz), F32)
     cells = COLS * nx * ny * nz
     solutions, gradient = pl.pallas_call(
@@ -461,9 +515,13 @@
             jax.ShapeDtypeStruct((COLS, nx, ny, nz), F32),
             jax.ShapeDtypeStruct((nx, ny, nz // nsrc), F32),
         ),
-        in_specs=[hbm, hbm, smem, smem, vmem, vmem],
+        in_specs=[hbm] * 6,
         out_specs=(hbm, vmem),
         scratch_shapes=[
+            pltpu.SMEM((count,), F32),
+            pltpu.SMEM((2, count), jnp.int32),
+            pltpu.VMEM((1, nrec), jnp.int32),
+            pltpu.VMEM((count, nrec), F32),
             block, block, block,
             pltpu.VMEM((3, 2, COLS, nx, nz), F32),
             pltpu.VMEM((3, 2, COLS, nx, nz), F32),
@@ -479,18 +537,19 @@
             pltpu.VMEM((group, 8, 128), F32),
             pltpu.VMEM((nsrc, nx, 8, 128), F32),
             pltpu.VMEM((nsrc - 1, nx, 8, 128), F32),
-            dma((2,)), dma,
-            dma((3, 4)), dma((3, 4)),
+            dma((6,)), dma,
+            dma((3, 2)), dma((3, 2)),
+            dma((3, 4, 2)), dma((3, 4, 2)),
             dma((4,)), dma((4,)),
             dma((group - 1,)), dma((group - 1,)),
-            dma((2, nsrc - 1)), dma((2, nsrc - 1)),
+            dma((8, nsrc - 1)), dma((8, nsrc - 1)),
         ],
         compiler_params=pltpu.CompilerParams(
-            collective_id=0, has_side_effects=True, vmem_limit_bytes=48 * 1024 * 1024
+            collective_id=0, has_side_effects=True, vmem_limit_bytes=64 * 1024 * 1024
         ),
         cost_estimate=pl.CostEstimate(flops=300 * cells, bytes_accessed=8 * cells, transcendentals=0),
     )(
-        warm_start.reshape((COLS, nx, ny, nz)), conductivity, currents, electrodes,
+        warm_start.reshape((COLS, nx, ny, nz)), conductivity, currents, electrodes.T,
         receivers.reshape(1, nrec), weights,
     )
     return solutions.reshape(warm_start.shape), gradient

time: 77 us -> 66.9 us (0.87)
  Pallas kernels: 69.5 us -> 60.7 us
  local copies, waits for them, and re-layouts: 6.54 us -> 5.39 us
    pallas_call x1, Pallas kernels: 69.5 us -> 60.7 us  [on_device(): pl.pallas_call(functools.partial(kernel, sizes), out_shape=(jax.ShapeDtyp...]
    unnamed x11 -> x4, local copies, waits for them, and re-layouts: 6.54 us -> 5.39 us
where the time goes in v1:
time: 66.9 us; the launch traced here: 66.8 us
  Pallas kernels  60.7 us (91%)
  local copies, waits for them, and re-layouts  5.39 us (8%)
    pallas_call x1, Pallas kernels, on_device(): pl.pallas_call(functools.partial(kernel, sizes), out_shape=(jax.ShapeDtyp...  60.7 us
    unnamed x4, local copies, waits for them, and re-layouts  5.39 us

profile of v1, /device:TPU:0, one launch (start us, length us, event | category | flops | bytes accessed | tf_op | source)
XLA Modules:
  0.0 66.8 jit_solution(15029838922515000605)
XLA Ops:
  0.6 60.7 %shard_map.77 = (f32[8,32,16,256]{3,2,1,0:T(8,128)}, f32[32,16,64]{2,1,0:T(8,128)}) custom-call(f32[8,32,16,256]{3,2,1,0:T(8,128)} %bitcast.4, f32[32,16,256]{2,1,0:T(8,128)} %cond.1, f32[4]{0:T(128)} %currents_in.1, s32[2,4]{1,0:T(2,128)} %bitcast.6, s32[1,256]{1,0:T(1,128)} %bitcast.7, f32[4,256]{1,0:T(4,128)} %weights_in.1), custom_call_target="tpu_custom_call" | custom-call | flops 314572800 | bytes 8388608 | tf_op jit(solution)/shard_map/pallas_call | solution.py:512
  61.4 0.0 copy-start
  61.4 4.7 %copy.10 = f32[2,4,32,16,256]{4,3,2,1,0:T(8,128)} copy(f32[2,4,32,16,256]{4,3,2,1,0:T(8,128)} %bitcast.5) | data formatting | bytes 8388608
  66.1 0.0 copy-done
  66.1 0.7 %copy.11 = f32[32,16,64]{2,1,0:T(8,128)} copy(f32[32,16,64]{2,1,0:T(8,128)S(1)} %copy-done) | data formatting | bytes 262144
Async XLA Ops:
  61.4 4.7 %copy-start = (f32[32,16,64]{2,1,0:T(8,128)S(1)}, f32[32,16,64]{2,1,0:T(8,128)}, u32[]{:S(2)}) copy-start(f32[32,16,64]{2,1,0:T(8,128)} %get-tuple-element.9) | copy-start | bytes 393220

commit v2 on v1

--- a/solution.py
+++ b/solution.py
@@ -512,8 +512,8 @@
     solutions, gradient = pl.pallas_call(
         functools.partial(kernel, sizes),
         out_shape=(
-            jax.ShapeDtypeStruct((COLS, nx, ny, nz), F32),
-            jax.ShapeDtypeStruct((nx, ny, nz // nsrc), F32),
+            pltpu.VMEM((COLS, nx, ny, nz), F32),
+            pltpu.VMEM((nx, ny, nz // nsrc), F32),
         ),
         in_specs=[hbm] * 6,
         out_specs=(hbm, vmem),
@@ -545,7 +545,7 @@
             dma((8, nsrc - 1)), dma((8, nsrc - 1)),
         ],
         compiler_params=pltpu.CompilerParams(
-            collective_id=0, has_side_effects=True, vmem_limit_bytes=64 * 1024 * 1024
+            collective_id=0, has_side_effects=True, vmem_limit_bytes=56 * 1024 * 1024
         ),
         cost_estimate=pl.CostEstimate(flops=300 * cells, bytes_accessed=8 * cells, transcendentals=0),
     )(

time: 66.9 us -> 63.8 us (0.954)
  local copies, waits for them, and re-layouts: 5.39 us -> 2.72 us
    unnamed x4 -> x2, local copies, waits for them, and re-layouts: 5.39 us -> 2.72 us
where the time goes in v2:
time: 63.8 us; the launch traced here: 63.7 us
  Pallas kernels  60.3 us (95%)
  local copies, waits for them, and re-layouts  2.72 us (4%)
  between operations  0.64 us (1%)
    pallas_call x1, Pallas kernels, on_device(): pl.pallas_call(functools.partial(kernel, sizes), out_shape=(pltpu.VMEM((C...  60.3 us
    unnamed x2, local copies, waits for them, and re-layouts  2.72 us

profile of v2, /device:TPU:0, one launch (start us, length us, event | category | flops | bytes accessed | tf_op | source)
XLA Modules:
  0.0 63.7 jit_solution(9831490945869864785)
XLA Ops:
  0.6 60.3 %shard_map.77 = (f32[8,32,16,256]{3,2,1,0:T(8,128)S(1)}, f32[32,16,64]{2,1,0:T(8,128)S(1)}) custom-call(f32[8,32,16,256]{3,2,1,0:T(8,128)} %bitcast.5, f32[32,16,256]{2,1,0:T(8,128)} %cond.1, f32[4]{0:T(128)} %currents_in.1, s32[2,4]{1,0:T(2,128)} %bitcast.6, s32[1,256]{1,0:T(1,128)} %bitcast.7, f32[4,256]{1,0:T(4,128)} %weights_in.1), custom_call_target="tpu_custom_call" | custom-call | flops 314572800 | bytes 8388608 | tf_op jit(solution)/shard_map/pallas_call | solution.py:512
  61.0 2.0 %copy.10 = f32[2,4,32,16,256]{4,3,2,1,0:T(8,128)} copy(f32[2,4,32,16,256]{4,3,2,1,0:T(8,128)S(1)} %bitcast.4) | data formatting | bytes 8388608
  63.0 0.7 %copy.11 = f32[32,16,64]{2,1,0:T(8,128)} copy(f32[32,16,64]{2,1,0:T(8,128)S(1)} %get-tuple-element.7) | data formatting | bytes 262144
